TPU v7x, 32 devices: a whole 2x2x4 slice. The times are simulated.
32 devices in a mesh: bx: 8 (over z, x), by: 4 (over y, core).
Axes of the slice: x: 2, y: 2, z: 4, core: 2. Of those that a mesh axis runs over, the one named last changes fastest.
Arguments:
- features: float32 [8, 4, 128, 128], P('bx', 'by'), may hold values from -6 to 6
- send_list: int32 [8, 4, 4, 32], P('bx', 'by'), may hold values from 0 to 127, as said below
- pair_first: int32 [8, 4, 2048], P('bx', 'by'), may hold values from 0 to 127, as said below
- pair_second: int32 [8, 4, 2048], P('bx', 'by'), may hold values from 0 to 255, as said below
- pair_species: int32 [8, 4, 2048], P('bx', 'by'), may hold values from 0 to 15
- pair_vector: float32 [8, 4, 3, 2048], P('bx', 'by'), may hold values from -2.5 to 2.5
- live_pairs: int32 [8, 4], P('bx', 'by'), may hold values from 1024 to 2048, as said below
- force_target: float32 [8, 4, 3, 128], P('bx', 'by'), may hold values from -12 to 12
- w_a: float32 [128, 512], replicated, may hold values from -0.5 to 0.5
- w_b: float32 [128, 512], replicated, may hold values from -0.5 to 0.5
- w_radial: float32 [8, 512], replicated, may hold values from -6 to 6
- species_table: float32 [16, 512], replicated, may hold values from -3 to 3
- w_mid: float32 [512, 512], replicated, may hold values from -0.25 to 0.25
- w_out: float32 [512], replicated, may hold values from -0.25 to 0.25
Outputs:
- forces: float32 [8, 4, 3, 128], P('bx', 'by')
- grad_w_a: float32 [128, 512], replicated
- grad_w_b: float32 [128, 512], replicated
- grad_w_radial: float32 [8, 512], replicated
- grad_species_table: float32 [16, 512], replicated
- grad_w_mid: float32 [512, 512], replicated
- grad_w_out: float32 [512], replicated
Inputs may be any that keep to these rules, and one draw needn't show every extreme that they name: `pair_first`: the first atom of a pair is a local atom of the brick. `pair_second`: below 128 a local atom other than the slot's first atom; 128 + d * 32 + g names ghost row g of direction d. `send_list`: for each brick and direction, 32 distinct local atoms. `live_pairs`: slots below it are live; in every draw some brick has all 2048 slots live.
All inputs are finite; a program needn't handle non-finite values.
Results may differ from a plain program's by a relative error of at most 0.0003.
Values sent between devices are 32-bit elements; how exact they have to be, the bound alone decides.
A program may use at most 64 MiB of HBM per device.

v0:
```python
import math

import jax
import jax.numpy as jnp
from jax import lax
from jax.sharding import PartitionSpec as P

PBLOCK = 256


RCUT = 5.0


def passed_along(block, axis, distance):
    devices = range(lax.axis_size(axis))
    route = [((i - distance) % len(devices), i) for i in devices]
    return lax.ppermute(block, axis, route)


def pair_slope(params, first_rows, second_rows, kinds, vec):
    w_a, w_b, w_radial, species_table, w_mid, w_out = params
    highest = lax.Precision.HIGHEST
    square = jnp.sum(vec * vec, axis=0) + 1.0
    radius = jnp.sqrt(square)
    order = (jnp.arange(1, w_radial.shape[0] + 1).astype(vec.dtype) * (math.pi / RCUT))[:, None]
    phase = order * radius[None, :]
    basis = jnp.sin(phase) / radius
    basis_slope = order * jnp.cos(phase) / radius - jnp.sin(phase) / square
    pre = jnp.dot(first_rows, w_a, precision=highest) + jnp.dot(second_rows, w_b, precision=highest)
    pre = (
        pre
        + jnp.dot(basis.T, w_radial, precision=highest)
        + jnp.dot(kinds, species_table, precision=highest)
    )
    sig_pre = jax.nn.sigmoid(pre)
    mid = jnp.dot(pre * sig_pre, w_mid, precision=highest)
    sig_mid = jax.nn.sigmoid(mid)
    grad_mid = w_out * sig_mid * (1.0 + mid * (1.0 - sig_mid))
    grad_pre = (
        jnp.dot(grad_mid, w_mid.T, precision=highest) * sig_pre * (1.0 + pre * (1.0 - sig_pre))
    )
    along = jnp.dot(grad_pre, w_radial.T, precision=highest)
    return jnp.sum(along.T * basis_slope, axis=0) / radius


def pull_x(value):
    return passed_along(value, "bx", -1)


def push_x(value):
    return passed_along(value, "bx", 1)


def pull_y(value):
    return passed_along(value, "by", -1)


def push_y(value):
    return passed_along(value, "by", 1)


def fetch_ghosts(rows):
    across = pull_x(jnp.stack([rows[0], rows[2], rows[3]]))
    upper = pull_y(jnp.stack([rows[1], across[1]]))
    lower = push_y(across[2])
    return jnp.stack([across[0], upper[0], upper[1], lower])


def return_partials(parts):
    upper = push_y(jnp.stack([parts[1], parts[2]]))
    lower = pull_y(parts[3])
    across = push_x(jnp.stack([parts[0], upper[1], lower]))
    return jnp.stack([across[0], upper[0], across[1], across[2]])


def sum_grads(grads):
    return lax.psum((grads[0], grads[1], grads[2], grads[3], grads[4], grads[5]), ("bx", "by"))


def local(
    features,
    send_list,
    pair_first,
    pair_second,
    pair_species,
    pair_vector,
    live_pairs,
    force_target,
    w_a,
    w_b,
    w_radial,
    species_table,
    w_mid,
    w_out,
):
    highest = lax.Precision.HIGHEST
    local_feat = features[0, 0]
    sends = send_list[0, 0]
    first = pair_first[0, 0]
    second = pair_second[0, 0]
    species = pair_species[0, 0]
    vectors = pair_vector[0, 0]
    live = live_pairs[0, 0]
    target = force_target[0, 0]
    atoms, width = local_feat.shape
    ghosts = sends.shape[1]
    extent = atoms + 4 * ghosts
    block_rows = PBLOCK
    params = (w_a, w_b, w_radial, species_table, w_mid, w_out)
    columns = jnp.arange(extent)
    kinds_all = jnp.arange(species_table.shape[0])
    slots = jnp.arange(block_rows)
    lent = jnp.take(local_feat, sends, axis=0)
    arrived = fetch_ghosts(lent)
    table = jnp.concatenate([local_feat, arrived.reshape(4 * ghosts, width)], axis=0)

    def block_inputs(block):
        start = block * block_rows
        fi = lax.dynamic_slice_in_dim(first, start, block_rows)
        se = lax.dynamic_slice_in_dim(second, start, block_rows)
        sp = lax.dynamic_slice_in_dim(species, start, block_rows)
        vec = lax.dynamic_slice_in_dim(vectors, start, block_rows, 1)
        kinds = (sp[:, None] == kinds_all[None, :]).astype(jnp.float32)
        alive = start + slots < live
        return (fi, se, kinds, vec, alive)

    def add_forces(block, total):
        fi, se, kinds, vec, alive = block_inputs(block)
        coupling = jnp.where(alive, pair_slope(params, table[fi], table[se], kinds, vec), 0.0)
        sign = (fi[:, None] == columns[None, :]).astype(jnp.float32) - (
            se[:, None] == columns[None, :]
        ).astype(jnp.float32)
        return total + jnp.dot(coupling[None, :] * vec, sign, precision=highest)

    blocks = (live + block_rows - 1) // block_rows
    extended = lax.fori_loop(0, blocks, add_forces, jnp.zeros((3, extent), jnp.float32))
    parts = jnp.transpose(extended[:, atoms:].reshape(3, 4, ghosts), (1, 0, 2))
    returned = return_partials(parts)
    onehot = (sends[:, :, None] == jnp.arange(atoms)[None, None, :]).astype(jnp.float32)
    forces = extended[:, :atoms] + jnp.einsum("dcg,dga->ca", returned, onehot, precision=highest)
    residual = (forces - target) / atoms
    residual_lent = jnp.transpose(jnp.take(residual, sends, axis=1), (1, 0, 2))
    residual_ghosts = fetch_ghosts(residual_lent)
    residual_table = jnp.concatenate(
        [residual, jnp.transpose(residual_ghosts, (1, 0, 2)).reshape(3, 4 * ghosts)], axis=1
    )

    def add_grads(block, carry):
        fi, se, kinds, vec, alive = block_inputs(block)
        weight = jnp.where(
            alive, jnp.sum((residual_table[:, fi] - residual_table[:, se]) * vec, axis=0), 0.0
        )
        first_rows = table[fi]
        second_rows = table[se]
        _, pull = jax.vjp(lambda p: pair_slope(p, first_rows, second_rows, kinds, vec), params)
        grads = pull(weight)[0]
        return jax.tree.map(lambda a, b: a + b, carry, grads)

    zero = jax.tree.map(jnp.zeros_like, params)
    summed = sum_grads(lax.fori_loop(0, blocks, add_grads, zero))
    return (forces[None, None], summed[0], summed[1], summed[2], summed[3], summed[4], summed[5])


def solution(mesh):
    return jax.shard_map(
        local,
        mesh=mesh,
        in_specs=(
            P("bx", "by", None, None),
            P("bx", "by", None, None),
            P("bx", "by", None),
            P("bx", "by", None),
            P("bx", "by", None),
            P("bx", "by", None, None),
            P("bx", "by"),
            P("bx", "by", None, None),
            P(),
            P(),
            P(),
            P(),
            P(),
            P(),
        ),
        out_specs=(P("bx", "by", None, None), P(), P(), P(), P(), P(), P()),
        check_vma=False,
    )
```

profile of v0, /device:TPU:0, one launch (start us, length us, event | category | flops | bytes accessed | tf_op | source)
XLA Modules:
  0.0 419.1 jit_solution(9590115850928197513)
XLA Ops:
  8.0 1.5 gather_fusion.6
  9.6 6.0 %collective-permute-start = (f32[3,32,128]{2,1,0:T(8,128)S(1)}, f32[3,32,128]{2,1,0:T(8,128)S(1)}, u32[]{:S(2)}, u32[]{:S(2)}) collective-permute-start(f32[3,32,128]{2,1,0:T(8,128)S(1)} %pad_maximum_fusion.2), channel_id=1, source_target_pairs={{4,0},{8,4},{12,8},{16,12},{20,16},{24,20},{28,24},{0,28},{5,1},{9... | collective-permute-start | bytes 147464 | tf_op jit(solution)/shard_map/ppermute | solution.py:17
  15.7 1.8 collective-permute-done
  18.8 2.2 collective-permute-done.2
  21.8 56.9 %while.35 = (s32[]{:T(128)}, f32[3,256]{1,0:T(4,128)S(1)}, s32[]{:T(128)}, s32[]{:T(128)}, f32[512]{0:T(512)S(1)}, /*index=5*/s32[2048]{0:T(1024)}, f32[256,128]...) while((s32[]{:T(128)}, f32[3,256]{1,0:T(4,128)S(1)}, ...), condition=%wide.region_3.4_spmd.clone.clone, body=%wide.region_0.3_spmd.clone.clone.sunk | while | flops 2069329408 | bytes 14536047 | solution.py:136
  27.2 1.1 fusion.258
  28.4 1.3 fusion.259
  36.7 1.1 fusion.258
  37.9 1.3 fusion.259
  46.2 1.1 fusion.258
  47.4 1.3 fusion.259
  55.7 1.2 fusion.258
  56.9 1.3 fusion.259
  66.3 1.3 fusion.259
  74.7 1.2 fusion.258
  75.8 1.3 fusion.259
  78.9 19.0 %collective-permute-start.4 = (f32[3,32]{1,0:T(4,128)S(1)}, f32[3,32]{1,0:T(4,128)S(1)}, u32[]{:S(2)}, u32[]{:S(2)}) collective-permute-start(f32[3,32]{1,0:T(4,128)S(1)} %get-tuple-element.579), channel_id=1, source_target_pairs={{1,0},{2,1},{3,2},{0,3},{5,4},{6,5},{7,6},{4,7},{9,8},{10,9},{11,1... | collective-permute-start | bytes 1160 | tf_op jit(solution)/shard_map/ppermute | solution.py:17
  97.9 1.2 collective-permute-done.3
  99.9 1.2 collective-permute-start.5
  101.0 6.4 %collective-permute-done.5 = f32[3,3,32]{2,1,0:T(4,128)S(1)} collective-permute-done((f32[3,3,32]{2,1,0:T(4,128)S(1)}, f32[3,3,32]{2,1,0:T(4,128)S(1)}, u32[]{:S(2)}, u32[]{:S(2)}) %collective-permute-start.5) | collective-permute-done | bytes 1184 | tf_op jit(solution)/shard_map/ppermute | solution.py:17
  109.3 2.1 collective-permute-start.6
  111.4 1.6 collective-permute-done.6
  113.6 2.6 collective-permute-done.8
  116.6 117.2 %while.34 = (s32[]{:T(128)}, f32[128,512]{1,0:T(8,128)S(1)}, f32[128,512]{1,0:T(8,128)S(1)}, f32[8,512]{1,0:T(8,128)S(1)}, f32[16,512]{1,0:T(8,128)S(1)}, /*inde...) while((s32[]{:T(128)}, f32[128,512]{1,0:T(8,128)S(1)}, ...), condition=%wide.region_8.9_spmd.clone, body=%wide.region_4.8_spmd.clone.sunk | while | flops 5753602048 | bytes 33315292 | solution.py:160
  125.4 1.2 fusion.234
  126.6 1.2 fusion.235
  128.4 1.3 multiply_reduce_fusion.5
  129.7 1.7 fusion.237
  133.2 1.4 fusion.240
  134.6 1.7 fusion.241
  144.9 1.2 fusion.234
  146.0 1.2 fusion.235
  147.9 1.3 multiply_reduce_fusion.5
  149.2 1.7 fusion.237
  152.6 1.4 fusion.240
  154.0 1.7 fusion.241
  164.3 1.2 fusion.234
  165.5 1.2 fusion.235
  167.3 1.3 multiply_reduce_fusion.5
  168.7 1.7 fusion.237
  172.1 1.4 fusion.240
  173.5 1.7 fusion.241
  183.8 1.2 fusion.234
  185.0 1.2 fusion.235
  186.8 1.3 multiply_reduce_fusion.5
  188.1 1.7 fusion.237
  191.6 1.4 fusion.240
  193.0 1.7 fusion.241
  203.3 1.2 fusion.234
  204.4 1.2 fusion.235
  206.3 1.3 multiply_reduce_fusion.5
  207.6 1.7 fusion.237
  211.0 1.4 fusion.240
  212.4 1.7 fusion.241
  222.7 1.2 fusion.234
  223.9 1.2 fusion.235
  225.7 1.3 multiply_reduce_fusion.5
  227.1 1.7 fusion.237
  230.5 1.4 fusion.240
  231.9 1.7 fusion.241
  235.5 78.9 %all-reduce = (f32[8,512]{1,0:T(8,128)}, f32[16,512]{1,0:T(8,128)}, f32[512]{0:T(512)}) all-reduce(f32[8,512]{1,0:T(8,128)S(1)} %get-tuple-element.268, f32[16,512]{1,0:T(8,128)S(1)} %get-tuple-element.269, f32[512]{0:T(512)S(1)} %get-tuple-element.271), channel_id=1, replica_groups=mesh['bx'=8,'by'=4] {'bx','by'}, use_global_device_ids=true, to_apply=%region_11.12 | all-reduce | flops 12800 | bytes 102400 | tf_op jit(solution)/shard_map/psum | solution.py:77
  314.5 93.3 %all-reduce.4.cloned.1.call-done = (f32[128,512]{1,0:T(8,128)}, f32[128,512]{1,0:T(8,128)}, f32[512,512]{1,0:T(8,128)}) async-done(((f32[128,512]{1,0:T(8,128)}, f32[128,512]{1,0:T(8,128)}, f32[512,512]{1,0:T(8,128)}), (f32[128,512]{1,0:T(8,128)}, f32[128,512]{1,0:T(8,128)}, f32[512,512]{1,0:T(8,128)})) %all-reduce.4.cloned.1.call-update) | async-done | bytes 1572880 | tf_op jit(solution)/shard_map/psum | solution.py:77
  407.8 1.8 copy.82
  409.6 1.7 copy.83
  (347 shorter events, 116.4 us)
Async XLA Ops:
  7.2 0.8 copy-start.10
  7.2 400.7 %all-reduce.4.cloned.1.call-start = ((), (), s32[]{:S(2)}) async-start(), calls=%async_computation | async-start | bytes 3145728 | tf_op jit(solution)/shard_map/psum | solution.py:77
  9.6 7.8 %collective-permute-start = (f32[3,32,128]{2,1,0:T(8,128)S(1)}, f32[3,32,128]{2,1,0:T(8,128)S(1)}, u32[]{:S(2)}, u32[]{:S(2)}) collective-permute-start(f32[3,32,128]{2,1,0:T(8,128)S(1)} %pad_maximum_fusion.2), channel_id=1, source_target_pairs={{4,0},{8,4},{12,8},{16,12},{20,16},{24,20},{28,24},{0,28},{5,1},{9... | collective-permute-start | bytes 147464 | tf_op jit(solution)/shard_map/ppermute | solution.py:17
  17.4 1.3 copy-start.9
  17.4 3.6 copy-start.5
  17.4 3.6 copy-start.13
  17.4 3.6 copy-start.1
  17.5 3.6 copy-start
  17.5 3.5 collective-permute-start.1
  17.6 3.3 collective-permute-start.2
  21.0 0.7 copy-start.4
  21.0 0.8 copy-start.7
  26.0 1.2 copy-start.11
  35.5 1.2 copy-start.11
  45.0 1.2 copy-start.11
  54.5 1.2 copy-start.11
  64.0 1.2 copy-start.11
  73.4 1.2 copy-start.11
  78.8 20.3 %collective-permute-start.3 = (f32[2,3,32]{2,1,0:T(4,128)S(1)}, f32[2,3,32]{2,1,0:T(4,128)S(1)}, u32[]{:S(2)}, u32[]{:S(2)}) collective-permute-start(f32[2,3,32]{2,1,0:T(4,128)S(1)} %stack.53), channel_id=1, source_target_pairs={{3,0},{0,1},{1,2},{2,3},{7,4},{4,5},{5,6},{6,7},{11,8},{8,9},{9,10... | collective-permute-start | bytes 2312 | tf_op jit(solution)/shard_map/ppermute | solution.py:17
  78.9 21.0 %collective-permute-start.4 = (f32[3,32]{1,0:T(4,128)S(1)}, f32[3,32]{1,0:T(4,128)S(1)}, u32[]{:S(2)}, u32[]{:S(2)}) collective-permute-start(f32[3,32]{1,0:T(4,128)S(1)} %get-tuple-element.579), channel_id=1, source_target_pairs={{1,0},{2,1},{3,2},{0,3},{5,4},{6,5},{7,6},{4,7},{9,8},{10,9},{11,1... | collective-permute-start | bytes 1160 | tf_op jit(solution)/shard_map/ppermute | solution.py:17
  99.9 7.6 %collective-permute-start.5 = (f32[3,3,32]{2,1,0:T(4,128)S(1)}, f32[3,3,32]{2,1,0:T(4,128)S(1)}, u32[]{:S(2)}, u32[]{:S(2)}) collective-permute-start(f32[3,3,32]{2,1,0:T(4,128)S(1)} %pad_maximum_fusion.4), channel_id=1, source_target_pairs={{28,0},{0,4},{4,8},{8,12},{12,16},{16,20},{20,24},{24,28},{29,1},{... | collective-permute-start | bytes 3464 | tf_op jit(solution)/shard_map/ppermute | solution.py:17
  107.5 0.7 copy-start.14
  109.3 3.7 collective-permute-start.6
  113.0 3.1 collective-permute-start.7
  113.1 3.1 collective-permute-start.8
  124.2 1.2 copy-start.12
  143.7 1.2 copy-start.12
  163.1 1.2 copy-start.12
  182.6 1.2 copy-start.12
  202.1 1.2 copy-start.12
  221.5 1.2 copy-start.12
  233.8 0.7 copy-start.2
  233.8 0.8 copy-start.3
  233.8 1.1 copy-start.6
  407.8 3.4 copy-start.8
Sparse Core Ops, SparseCore 0:
  235.1 172.6 all-reduce.3
where the time goes:
time: 421 us; the launch traced here: 419 us
  matrix products  117 us (28%)
  waiting for transfers between devices  110 us (26%)
  blocking collectives  78.9 us (19%)
  local copies, waits for them, and re-layouts  47.4 us (11%)
  starting transfers between devices  29.5 us (7%)
  other arithmetic  19.6 us (5%)
  between operations  15.1 us (4%)
    psum x1, waiting for transfers between devices, sum_grads(): lax.psum((grads[0], grads[1], grads[2], grads[3], grads[4], grads[5]), ('...  93.3 us
    psum x1, blocking collectives, sum_grads(): lax.psum((grads[0], grads[1], grads[2], grads[3], grads[4], grads[5]), ('...  78.9 us
    dot_general x24, matrix products, pair_slope(): mid = jnp.dot(pre * sig_pre, w_mid, precision=highest)  33.9 us
    dot_general x24, matrix products, pair_slope(): jnp.dot(grad_mid, w_mid.T, precision=highest) * sig_pre  31.7 us
    ppermute x9, starting transfers between devices, passed_along(): return lax.ppermute(block, axis, route)  29.4 us
    ppermute x9, waiting for transfers between devices, passed_along(): return lax.ppermute(block, axis, route)  16.6 us
    dot_general x18, matrix products, pair_slope(): jnp.dot(basis.T, w_radial, precision=highest)  11.3 us
    dot_general x18, matrix products, pair_slope(): along = jnp.dot(grad_pre, w_radial.T, precision=highest)  11.1 us
  transfers between devices with their start and end apart: 10, of which 8 were waited for; matrix products, arithmetic and copies ran while one was open for 0% of the time, Pallas kernels for 0%

commit v1 on v0

v1 whole, which is shorter than its diff:
```python
import functools
import math

import jax
import jax.numpy as jnp
from jax import lax
from jax.experimental import pallas as pl
from jax.experimental.pallas import tpu as pltpu
from jax.sharding import PartitionSpec as P

PBLOCK = 256
LANES = 128
RCUT = 5.0
CHUNK = 64
VMEM_BYTES = 56 * 1024 * 1024
MESH = pl.DeviceIdType.MESH
HIGHEST = lax.Precision.HIGHEST
F32 = jnp.float32
BF16 = jnp.bfloat16


def passed_along(block, axis, distance):
    devices = range(lax.axis_size(axis))
    route = [((i - distance) % len(devices), i) for i in devices]
    return lax.ppermute(block, axis, route)


def pull_x(value):
    return passed_along(value, "bx", -1)


def push_x(value):
    return passed_along(value, "bx", 1)


def pull_y(value):
    return passed_along(value, "by", -1)


def push_y(value):
    return passed_along(value, "by", 1)


def fetch_ghosts(rows):
    across = pull_x(jnp.stack([rows[0], rows[2], rows[3]]))
    upper = pull_y(jnp.stack([rows[1], across[1]]))
    lower = push_y(across[2])
    return jnp.stack([across[0], upper[0], upper[1], lower])


def return_partials(parts):
    upper = push_y(jnp.stack([parts[1], parts[2]]))
    lower = pull_y(parts[3])
    across = push_x(jnp.stack([parts[0], upper[1], lower]))
    return jnp.stack([across[0], upper[0], across[1], across[2]])


def split(x):
    hi = x.astype(BF16)
    return hi, (x - hi.astype(F32)).astype(BF16)


def mm(a, b):
    return jnp.dot(a, b, preferred_element_type=F32)


def mm_t(a, b):
    return lax.dot_general(a, b, (((1,), (1,)), ((), ())), preferred_element_type=F32)


def round_up(n, k):
    return -(-n // k) * k


def onehot(ids, rows, cols):
    return jnp.where(lax.broadcasted_iota(jnp.int32, (rows, cols), 0) == ids, 1.0, 0.0).astype(BF16)


def slopes_of(z):
    sig = 0.5 * jnp.tanh(0.5 * z) + 0.5
    rest = 1.0 - sig
    act = z * sig
    d1 = sig + act * rest
    d2 = sig * rest * (2.0 + z * rest - act)
    return act, d1, d2


def phase_one(
    atoms,
    live, first, second, species, vec, table, w_a, w_b, w_radial, species_table, w_mid, w_out,
    ext, m1, mt, u_hi, u_lo, eg, zt, xs,
    c_hi, c_lo, wt_hi, wt_lo, w_hi, w_lo, wo, za, ta, md, eg_hi, eg_lo, wide,
):
    step = pl.program_id(0)
    extent, width = table.shape
    hidden = w_mid.shape[0]
    nb, ns = w_radial.shape[0], species_table.shape[0]
    pb = first.shape[1]
    base = atoms + extent
    used = base + 2 * nb + ns

    @pl.when(step == 0)
    def _():
        wide[...] = jnp.zeros_like(wide)
        wide[0:atoms, :] = jnp.dot(table[0:atoms, :], w_a[...], precision=HIGHEST, preferred_element_type=F32)
        wide[atoms:base, :] = jnp.dot(table[...], w_b[...], precision=HIGHEST, preferred_element_type=F32)
        wide[base : base + nb, :] = w_radial[...]
        wide[base + nb : base + 2 * nb, :] = w_radial[...]
        wide[base + 2 * nb : used, :] = species_table[...]
        c_hi[...], c_lo[...] = split(wide[...].T)
        w_hi[...], w_lo[...] = split(w_mid[...])
        wt_hi[...], wt_lo[...] = split(w_mid[...].T)
        wo[...] = jnp.broadcast_to(w_out[...], (pb, hidden)).T
        ext[...] = jnp.zeros_like(ext)

    square = jnp.sum(vec[...] * vec[...], axis=0, keepdims=True) + 1.0
    radius = jnp.sqrt(square)
    order = (lax.broadcasted_iota(jnp.int32, (nb, pb), 0) + 1).astype(F32) * (math.pi / RCUT)
    phase = order * radius
    sine, cosine = jnp.sin(phase), jnp.cos(phase)
    basis = sine / radius
    slope_basis = (order * cosine / radius - sine / square) / radius
    basis_hi = basis.astype(BF16).astype(F32)
    slope_hi = slope_basis.astype(BF16).astype(F32)
    m1[0:atoms, :] = onehot(first[...], atoms, pb)
    m1[atoms:base, :] = onehot(second[...], extent, pb)
    m1[base : base + 2 * nb, :] = jnp.concatenate([basis_hi, basis - basis_hi], axis=0).astype(BF16)
    m1[base + 2 * nb : used, :] = onehot(species[...], ns, pb)
    m1[used:, :] = jnp.zeros((m1.shape[0] - used, pb), BF16)
    mt[0 : 2 * nb, :] = jnp.concatenate([slope_hi, slope_basis - slope_hi], axis=0).astype(BF16)
    mt[2 * nb :, :] = jnp.zeros((mt.shape[0] - 2 * nb, pb), BF16)

    za[...] = mm(c_hi[...], m1[...]) + mm(c_lo[...], m1[...])
    ta[...] = mm(c_hi[:, base:], mt[...]) + mm(c_lo[:, base:], mt[...])
    for i in range(0, hidden, CHUNK):
        rows = slice(i, i + CHUNK)
        z, t = za[rows, :], ta[rows, :]
        act, d1, d2 = slopes_of(z)
        za[rows, :] = d1
        ta[rows, :] = d2 * t
        u_hi[rows, 0:pb], u_lo[rows, 0:pb] = split(act)
        u_hi[rows, pb:], u_lo[rows, pb:] = split(d1 * t)
    md[...] = mm(wt_hi[...], u_hi[...]) + mm(wt_lo[...], u_hi[...]) + mm(wt_hi[...], u_lo[...])
    slope = jnp.zeros((1, pb), F32)
    for i in range(0, hidden, CHUNK):
        rows = slice(i, i + CHUNK)
        m, dm, out = md[rows, 0:pb], md[rows, pb:], wo[rows, :]
        _, d1, d2 = slopes_of(m)
        x = d1 * dm
        xs[rows, :] = x
        slope = slope + jnp.sum(out * x, axis=0, keepdims=True)
        e, g = out * d2 * dm, out * d1
        eg[rows, 0:pb] = e
        eg[rows, pb:] = g
        eg_hi[rows, 0:pb], eg_lo[rows, 0:pb] = split(e)
        eg_hi[rows, pb:], eg_lo[rows, pb:] = split(g)
    md[...] = mm(w_hi[...], eg_hi[...]) + mm(w_lo[...], eg_hi[...]) + mm(w_hi[...], eg_lo[...])
    for i in range(0, hidden, CHUNK):
        rows = slice(i, i + CHUNK)
        e, g, d1 = md[rows, 0:pb], md[rows, pb:], za[rows, :]
        zt[rows, 0:pb] = e * d1 + g * ta[rows, :]
        zt[rows, pb:] = g * d1
    slots = step * pb + lax.broadcasted_iota(jnp.int32, (1, pb), 1)
    coupling = jnp.where(slots < live[0, 0], slope, 0.0)
    pushed = coupling * vec[...]
    pushed_hi = pushed.astype(BF16).astype(F32)
    pushed2 = jnp.concatenate([pushed_hi, pushed - pushed_hi], axis=0).astype(BF16)
    half = pushed.shape[0]
    on_first = mm_t(pushed2, m1[0:atoms, :])
    on_second = mm_t(pushed2, m1[atoms:base, :])
    ext[:, 0:atoms] += on_first[0:half] + on_first[half:]
    ext[...] -= on_second[0:half] + on_second[half:]


def phase_two(
    atoms, nb, ns,
    live, first, vec, table, residual, m1, mt, u_hi, u_lo, eg, zt, xs,
    grads,
    we_hi, we_lo, zh, zl, th, tl, d_mid, d_wide, d_slope, d_out,
):
    step = pl.program_id(0)
    extent, width = table.shape
    hidden = u_hi.shape[0]
    pb = first.shape[1]
    base = atoms + extent

    @pl.when(step == 0)
    def _():
        d_mid[...] = jnp.zeros_like(d_mid)
        d_wide[...] = jnp.zeros_like(d_wide)
        d_slope[...] = jnp.zeros_like(d_slope)
        d_out[...] = jnp.zeros_like(d_out)

    res = residual[...]
    res_hi = res.astype(BF16).astype(F32)
    res2 = jnp.concatenate([res_hi, res - res_hi], axis=0).astype(BF16)
    half = res.shape[0]
    apart = mm(res2[:, 0:atoms], m1[0:atoms, :]) - mm(res2, m1[atoms:base, :])
    slots = step * pb + lax.broadcasted_iota(jnp.int32, (1, pb), 1)
    pulled = jnp.sum((apart[0:half] + apart[half:]) * vec[...], axis=0, keepdims=True)
    weight = jnp.where(slots < live[0, 0], pulled, 0.0)
    for i in range(0, hidden, CHUNK):
        rows = slice(i, i + CHUNK)
        we_hi[rows, 0:pb], we_lo[rows, 0:pb] = split(eg[rows, 0:pb] * weight)
        we_hi[rows, pb:], we_lo[rows, pb:] = split(eg[rows, pb:] * weight)
        zh[rows, :], zl[rows, :] = split(zt[rows, 0:pb] * weight)
        th[rows, :], tl[rows, :] = split(zt[rows, pb:] * weight)
        x = xs[rows, :] * weight
        total = d_out[rows, :]
        for j in range(0, pb, LANES):
            total = total + x[:, j : j + LANES]
        d_out[rows, :] = total
    d_mid[...] += mm_t(u_hi[...], we_hi[...]) + mm_t(u_lo[...], we_hi[...]) + mm_t(u_hi[...], we_lo[...])
    d_wide[...] += mm_t(m1[...], zh[...]) + mm_t(m1[...], zl[...])
    d_slope[...] += mm_t(mt[0 : 2 * nb, :], th[...]) + mm_t(mt[0 : 2 * nb, :], tl[...])

    @pl.when(step == pl.num_programs(0) - 1)
    def _():
        across = table[...].T
        d_a = jnp.dot(across[:, 0:atoms], d_wide[0:atoms, :], precision=HIGHEST, preferred_element_type=F32)
        d_b = jnp.dot(across, d_wide[atoms:base, :], precision=HIGHEST, preferred_element_type=F32)
        d_radial = (
            d_wide[base : base + nb, :] + d_wide[base + nb : base + 2 * nb, :]
            + d_slope[0:nb, :] + d_slope[nb:, :]
        )
        d_species = d_wide[base + 2 * nb : base + 2 * nb + ns, :]
        d_last = jnp.broadcast_to(jnp.sum(d_out[...].T, axis=0, keepdims=True), (8, hidden))
        at = 0
        for piece in (d_a, d_b, d_mid[...], d_species, d_radial, d_last):
            n = piece.shape[0]
            for j in range(grads.shape[0]):
                grads[j, at : at + n, :] = piece[:, j * LANES : (j + 1) * LANES]
            at += n
        if at < grads.shape[1]:
            grads[:, at:, :] = jnp.zeros((grads.shape[0], grads.shape[1] - at, LANES), F32)


def unpack(packed, *outs):
    at = 0
    for out in outs:
        n = out.shape[0]
        for j in range(packed.shape[0]):
            out[:, j * LANES : (j + 1) * LANES] = packed[j, at : at + n, :]
        at += n


def sum_kernel(sizes, cut, mine, out, acc, from_core, in_a, in_b, in_c, in_d, in_z, send, recv):
    gc, gx, gy, gz = sizes
    bx, by = lax.axis_index("bx"), lax.axis_index("by")
    c, y = lax.rem(by, gc), lax.div(by, gc)
    x, z = lax.rem(bx, gx), lax.div(bx, gx)

    def place(px, pz, py, pc):
        return (pz * gx + px, py * gc + pc)

    def peers(me, size):
        return [(k, lax.rem(me + k, size)) for k in range(1, size)]

    cores = [(k, p, place(x, z, y, p)) for k, p in peers(c, gc)]
    xs = [(k, p, place(p, z, y, c)) for k, p in peers(x, gx)]
    ys = [(k, p, place(x, z, p, c)) for k, p in peers(y, gy)]
    zs = [(k, p, place(x, p, y, c)) for k, p in peers(z, gz)]
    everyone = cores + xs + ys + zs
    barrier = pltpu.get_barrier_semaphore()
    for _, _, device in everyone:
        pl.semaphore_signal(barrier, inc=1, device_id=device, device_id_type=MESH)
    pl.semaphore_wait(barrier, len(everyone))
    count = [0]

    def go(src, dst, device):
        slot = count[0]
        count[0] += 1
        copy = pltpu.make_async_remote_copy(
            src_ref=src, dst_ref=dst, send_sem=send.at[slot], recv_sem=recv.at[slot],
            device_id=device, device_id_type=MESH,
        )
        copy.start()
        return copy

    def finish(copies):
        for copy in copies:
            copy.wait()

    lower, upper = pl.ds(0, cut), pl.ds(cut, acc.shape[3] - cut)
    finish([go(mine.at[p], from_core.at[k - 1], d) for k, p, d in cores])
    total = mine[c]
    for k in range(gc - 1):
        total = total + from_core[k]
    acc[...] = total
    first = [go(acc.at[p, :, :, lower], in_a.at[k - 1], d) for k, p, d in xs]
    other = [go(acc.at[:, p, :, upper], in_b.at[k - 1], d) for k, p, d in ys]
    finish(first)
    for k in range(gx - 1):
        acc[x, :, :, lower] += in_a[k]
    first = [go(acc.at[x, p, :, lower], in_c.at[k - 1], d) for k, p, d in ys]
    finish(other)
    for k in range(gy - 1):
        acc[:, y, :, upper] += in_b[k]
    other = [go(acc.at[p, y, :, upper], in_d.at[k - 1], d) for k, p, d in xs]
    finish(first)
    for k in range(gy - 1):
        acc[x, y, :, lower] += in_c[k]
    finish(other)
    for k in range(gx - 1):
        acc[x, y, :, upper] += in_d[k]
    finish([go(acc.at[x, y, p], in_z.at[k - 1], d) for k, p, d in zs])
    total = acc[x, y, z]
    for k in range(gz - 1):
        total = total + in_z[k]
    out[c, x, y, z] = total
    finish([go(out.at[c, x, y, z], out.at[c, x, y, z], d) for k, p, d in zs])
    here = out.at[c, x, y, :, lower]
    first = [go(here, here, d) for k, p, d in ys]
    here = out.at[c, x, y, :, upper]
    other = [go(here, here, d) for k, p, d in xs]
    finish(first)
    here = out.at[c, x, :, :, lower]
    first = [go(here, here, d) for k, p, d in xs]
    finish(other)
    here = out.at[c, :, y, :, upper]
    other = [go(here, here, d) for k, p, d in ys]
    finish(first)
    finish(other)
    finish([go(out.at[c], out.at[c], d) for k, p, d in cores])


def sum_everywhere(packed, sizes, rows):
    gc, gx, gy, gz = sizes
    cut = (rows // 8 + 1) // 2 * 8
    n_copies = 2 * (gc - 1) + 4 * (gx - 1) + 4 * (gy - 1) + 2 * (gz - 1)
    shape = (gc, gx, gy, gz, rows, LANES)

    def room(*dims):
        return pltpu.VMEM(tuple(max(d, 1) for d in dims) + (LANES,), F32)

    whole = pl.BlockSpec(memory_space=pltpu.VMEM)
    return pl.pallas_call(
        functools.partial(sum_kernel, sizes, cut),
        out_shape=jax.ShapeDtypeStruct(shape, F32),
        in_specs=[whole],
        out_specs=whole,
        scratch_shapes=[
            room(gx, gy, gz, rows),
            room(gc - 1, gx, gy, gz, rows),
            room(gx - 1, gy, gz, cut),
            room(gy - 1, gx, gz, rows - cut),
            room(gy - 1, gz, cut),
            room(gx - 1, gz, rows - cut),
            room(gz - 1, rows),
            pltpu.SemaphoreType.DMA((n_copies,)),
            pltpu.SemaphoreType.DMA((n_copies,)),
        ],
        compiler_params=pltpu.CompilerParams(
            collective_id=1, has_side_effects=True, vmem_limit_bytes=VMEM_BYTES
        ),
        name="sum_grads",
    )(packed.reshape(shape))


def local(
    features,
    send_list,
    pair_first,
    pair_second,
    pair_species,
    pair_vector,
    live_pairs,
    force_target,
    w_a,
    w_b,
    w_radial,
    species_table,
    w_mid,
    w_out,
):
    local_feat = features[0, 0]
    sends = send_list[0, 0]
    first, second, species = pair_first[0], pair_second[0], pair_species[0]
    vec = jnp.pad(pair_vector[0, 0], ((0, 5), (0, 0)))
    target = force_target[0, 0]
    atoms, width = local_feat.shape
    ghosts = sends.shape[1]
    extent = atoms + 4 * ghosts
    hidden = w_mid.shape[0]
    nb, ns = w_radial.shape[0], species_table.shape[0]
    pairs = first.shape[1]
    pb = min(PBLOCK, pairs)
    steps = pairs // pb
    deep = round_up(atoms + extent + 2 * nb + ns, LANES)
    thin = deep - atoms - extent

    lent = jnp.take(local_feat, sends, axis=0)
    arrived = fetch_ghosts(lent)
    table = jnp.concatenate([local_feat, arrived.reshape(4 * ghosts, width)], axis=0)

    smem = pl.BlockSpec(memory_space=pltpu.SMEM)

    def full(*dims):
        return pl.BlockSpec(dims, lambda i: (0,) * len(dims))

    def lane_block(rows):
        return pl.BlockSpec((rows, pb), lambda i: (0, i))

    def step_block(rows, cols):
        return pl.BlockSpec((None, rows, cols), lambda i: (i, 0, 0))

    def stacked(rows, cols, dtype):
        return jax.ShapeDtypeStruct((steps, rows, cols), dtype)

    params = pltpu.CompilerParams(
        dimension_semantics=("arbitrary",), vmem_limit_bytes=VMEM_BYTES
    )
    kept_specs = [
        step_block(deep, pb),
        step_block(thin, pb),
        step_block(hidden, 2 * pb),
        step_block(hidden, 2 * pb),
        step_block(hidden, 2 * pb),
        step_block(hidden, 2 * pb),
        step_block(hidden, pb),
    ]
    ext, *kept = pl.pallas_call(
        functools.partial(phase_one, atoms),
        grid=(steps,),
        out_shape=[
            jax.ShapeDtypeStruct((8, extent), F32),
            stacked(deep, pb, BF16),
            stacked(thin, pb, BF16),
            stacked(hidden, 2 * pb, BF16),
            stacked(hidden, 2 * pb, BF16),
            stacked(hidden, 2 * pb, F32),
            stacked(hidden, 2 * pb, F32),
            stacked(hidden, pb, F32),
        ],
        in_specs=[
            smem,
            lane_block(1),
            lane_block(1),
            lane_block(1),
            lane_block(8),
            full(extent, width),
            full(width, hidden),
            full(width, hidden),
            full(nb, hidden),
            full(ns, hidden),
            full(hidden, hidden),
            full(1, hidden),
        ],
        out_specs=[full(8, extent)] + kept_specs,
        scratch_shapes=[
            pltpu.VMEM((hidden, deep), BF16),
            pltpu.VMEM((hidden, deep), BF16),
            pltpu.VMEM((hidden, hidden), BF16),
            pltpu.VMEM((hidden, hidden), BF16),
            pltpu.VMEM((hidden, hidden), BF16),
            pltpu.VMEM((hidden, hidden), BF16),
            pltpu.VMEM((hidden, pb), F32),
            pltpu.VMEM((hidden, pb), F32),
            pltpu.VMEM((hidden, pb), F32),
            pltpu.VMEM((hidden, 2 * pb), F32),
            pltpu.VMEM((hidden, 2 * pb), BF16),
            pltpu.VMEM((hidden, 2 * pb), BF16),
            pltpu.VMEM((deep, hidden), F32),
        ],
        compiler_params=params,
        name="edge_forward",
    )(
        live_pairs, first, second, species, vec, table, w_a, w_b, w_radial, species_table, w_mid,
        w_out[None],
    )
    extended = ext[:3]
    parts = jnp.transpose(extended[:, atoms:].reshape(3, 4, ghosts), (1, 0, 2))
    returned = return_partials(parts)
    spots = (sends[:, :, None] == jnp.arange(atoms)[None, None, :]).astype(jnp.float32)
    forces = extended[:, :atoms] + jnp.einsum("dcg,dga->ca", returned, spots, precision=HIGHEST)
    residual = (forces - target) / atoms
    residual_lent = jnp.transpose(jnp.take(residual, sends, axis=1), (1, 0, 2))
    residual_ghosts = fetch_ghosts(residual_lent)
    residual_table = jnp.concatenate(
        [residual, jnp.transpose(residual_ghosts, (1, 0, 2)).reshape(3, 4 * ghosts)], axis=1
    )

    nbx, nby = lax.axis_size("bx"), lax.axis_size("by")
    gx = 2 if nbx % 2 == 0 else 1
    gc = 2 if nby % 2 == 0 else 1
    sizes = (gc, gx, nby // gc, nbx // gx)
    devices = nbx * nby
    columns = hidden // LANES
    body = 2 * width + hidden + ns + nb + 8
    rows = round_up(-(-body * columns // devices), 8)
    while devices * rows % (8 * columns):
        rows += 8
    tall = devices * rows // columns
    packed = pl.pallas_call(
        functools.partial(phase_two, atoms, nb, ns),
        grid=(steps,),
        out_shape=jax.ShapeDtypeStruct((columns, tall, LANES), F32),
        in_specs=[smem, lane_block(1), lane_block(8), full(extent, width), full(8, extent)]
        + kept_specs,
        out_specs=full(columns, tall, LANES),
        scratch_shapes=[
            pltpu.VMEM((hidden, 2 * pb), BF16),
            pltpu.VMEM((hidden, 2 * pb), BF16),
            pltpu.VMEM((hidden, pb), BF16),
            pltpu.VMEM((hidden, pb), BF16),
            pltpu.VMEM((hidden, pb), BF16),
            pltpu.VMEM((hidden, pb), BF16),
            pltpu.VMEM((hidden, hidden), F32),
            pltpu.VMEM((deep, hidden), F32),
            pltpu.VMEM((2 * nb, hidden), F32),
            pltpu.VMEM((hidden, LANES), F32),
        ],
        compiler_params=params,
        name="edge_backward",
    )(live_pairs, first, vec, table, jnp.pad(residual_table, ((0, 5), (0, 0))), *kept)
    summed = sum_everywhere(packed, sizes, rows).reshape(columns, tall, LANES)
    outs = pl.pallas_call(
        unpack,
        out_shape=[
            jax.ShapeDtypeStruct((n, hidden), F32) for n in (width, width, hidden, ns, nb, 8)
        ],
        compiler_params=pltpu.CompilerParams(vmem_limit_bytes=VMEM_BYTES),
        name="unpack_grads",
    )(summed)
    d_a, d_b, d_mid, d_species, d_radial, d_out = outs
    return (forces[None, None], d_a, d_b, d_radial, d_species, d_mid, d_out[0])


def solution(mesh):
    return jax.shard_map(
        local,
        mesh=mesh,
        in_specs=(
            P("bx", "by", None, None),
            P("bx", "by", None, None),
            P("bx", "by", None),
            P("bx", "by", None),
            P("bx", "by", None),
            P("bx", "by", None, None),
            P("bx", "by"),
            P("bx", "by", None, None),
            P(),
            P(),
            P(),
            P(),
            P(),
            P(),
        ),
        out_specs=(P("bx", "by", None, None), P(), P(), P(), P(), P(), P()),
        check_vma=False,
    )
```

time: 421 us -> 140 us (0.33)
  matrix products: 117 us -> 0.92 us
  Pallas kernels: 0 us -> 102 us
  waiting for transfers between devices: 110 us -> 14 us
  blocking collectives: 78.9 us -> 0 us
  local copies, waits for them, and re-layouts: 47.4 us -> 6.59 us
  starting transfers between devices: 29.5 us -> 11.2 us
  other arithmetic: 19.6 us -> 3.63 us
  between operations: 15.1 us -> 1.4 us
    dot_general x145 -> x1, matrix products: 117 us -> 0.92 us  [local(): jnp.einsum('dcg,dga->ca', returned, spots, precision=HIGHEST)]
    pallas_call x0 -> x4, Pallas kernels: none -> 102 us  [the longest x1 42.7 us: sum_everywhere(): pl.pallas_call(functools.partial(sum_kernel, sizes, cut), out_shape=jax.S...]
    psum x1 -> x0, waiting for transfers between devices: 93.3 us -> none  [sum_grads(): lax.psum((grads[0], grads[1], grads[2], grads[3], grads[4], grads[5]), ('...]
    psum x1 -> x0, blocking collectives: 78.9 us -> none  [sum_grads(): lax.psum((grads[0], grads[1], grads[2], grads[3], grads[4], grads[5]), ('...]
    gather x36 -> x0, local copies, waits for them, and re-layouts: 26.3 us -> none  [the longest x6 4.41 us: add_grads(): second_rows = table[se]]
    ppermute x9, starting transfers between devices: 29.4 us -> 11.2 us  [passed_along(): return lax.ppermute(block, axis, route)]
    select_n x18 -> x0, other arithmetic: 13.3 us -> none  [the longest x6 4.7 us: add_forces(): table[se]]
    dynamic_slice x24 -> x0, local copies, waits for them, and re-layouts: 10 us -> none  [the longest x12 9.17 us: block_inputs(): sp = lax.dynamic_slice_in_dim(species, start, block_rows)]
  transfers between devices with their start and end apart: 10 -> 9, of which waited for: 8 -> 6; matrix products, arithmetic and copies ran while one was open for 0% -> 1% of each run, Pallas kernels for 0% -> 0%
where the time goes in v1:
time: 140 us
  Pallas kernels  102 us (73%)
  waiting for transfers between devices  14 us (10%)
  starting transfers between devices  11.2 us (8%)
  local copies, waits for them, and re-layouts  6.59 us (5%)
  other arithmetic  3.63 us (3%)
    pallas_call x1, Pallas kernels, sum_everywhere(): pl.pallas_call(functools.partial(sum_kernel, sizes, cut), out_shape=jax.S...  42.7 us
    pallas_call x1, Pallas kernels, local(): pl.pallas_call(functools.partial(phase_one, atoms), grid=(steps,), out_sh...  37.5 us
    pallas_call x1, Pallas kernels, local(): pl.pallas_call(functools.partial(phase_two, atoms, nb, ns), grid=(steps,)...  19.2 us
    ppermute x9, waiting for transfers between devices, passed_along(): return lax.ppermute(block, axis, route)  14 us
    ppermute x9, starting transfers between devices, passed_along(): return lax.ppermute(block, axis, route)  11.2 us
  transfers between devices with their start and end apart: 9, of which 6 were waited for; matrix products, arithmetic and copies ran while one was open for 1% of the time, Pallas kernels for 0%

profile of v1, /device:TPU:0, one launch (start us, length us, event | category | flops | bytes accessed | tf_op | source)
XLA Modules:
  0.0 139.8 jit_solution(7565717520757570112)
XLA Ops:
  0.6 0.7 compare_and_fusion
  1.3 0.7 compare_select_fusion
  2.0 0.1 reshape.71
  2.1 1.5 %gather_fusion = f32[128,128]{1,0:T(8,128)S(1)} fusion(f32[128,128]{1,0:T(8,128)} %bitcast.47, s32[1024]{0:T(1024)S(1)} %pad_clamp_fusion), kind=kCustom, calls=%fused_computation | custom fusion | bytes 131584 | tf_op jit(solution)/shard_map/jit(_take)/gather | solution.py:392
  3.6 0.1 broadcast_select_fusion
  3.7 6.0 %collective-permute-start = (f32[3,32,128]{2,1,0:T(8,128)S(1)}, f32[3,32,128]{2,1,0:T(8,128)S(1)}, u32[]{:S(2)}, u32[]{:S(2)}) collective-permute-start(f32[3,32,128]{2,1,0:T(8,128)S(1)} %pad_maximum_fusion.2), channel_id=1, source_target_pairs={{4,0},{8,4},{12,8},{16,12},{20,16},{24,20},{28,24},{0,28},{5,1},{9... | collective-permute-start | bytes 147464 | tf_op jit(solution)/shard_map/ppermute | solution.py:25
  9.7 1.8 %collective-permute-done = f32[3,32,128]{2,1,0:T(8,128)S(1)} collective-permute-done((f32[3,32,128]{2,1,0:T(8,128)S(1)}, f32[3,32,128]{2,1,0:T(8,128)S(1)}, u32[]{:S(2)}, u32[]{:S(2)}) %collective-permute-start) | collective-permute-done | bytes 49184 | tf_op jit(solution)/shard_map/ppermute | solution.py:25
  11.5 0.2 collective-permute-start.1
  11.7 0.4 collective-permute-start.2
  12.7 0.8 copy.31
  13.5 0.6 pad.8.vec
  14.1 0.9 collective-permute-done.2
  15.0 0.0 collective-permute-done.1
  15.0 1.5 %pad_maximum_fusion.table = f32[256,128]{1,0:T(8,128)} fusion(f32[128,128]{1,0:T(8,128)S(1)} %bitcast.50, f32[128,128]{1,0:T(8,128)} %bitcast.48), kind=kLoop, calls=%fused_computation.4 | loop fusion | flops 32768 | bytes 262144 | tf_op jit(solution)/shard_map/concatenate | solution.py:394
  16.5 37.5 %edge_forward.1 = (f32[8,256]{1,0:T(8,128)}, bf16[8,512,256]{2,1,0:T(8,128)(2,1)}, bf16[8,128,256]{2,1,0:T(8,128)(2,1)}, bf16[8,512,512]{2,1,0:T(8,128)(2,1)}, b...) custom-call(s32[1,1]{1,0:T(1,128)S(6)} %copy.33.live, ...), custom_call_target="tpu_custom_call" | custom-call | tf_op jit(solution)/shard_map/edge_forward/pallas_call | solution.py:422
  54.1 0.7 slice.88
  54.8 0.1 reshape.65
  54.9 0.3 collective-permute-start.3
  55.2 1.4 %collective-permute-start.4 = (f32[3,32]{1,0:T(4,128)S(1)}, f32[3,32]{1,0:T(4,128)S(1)}, u32[]{:S(2)}, u32[]{:S(2)}) collective-permute-start(f32[3,32]{1,0:T(4,128)S(1)} %get-tuple-element.50), channel_id=1, source_target_pairs={{1,0},{2,1},{3,2},{0,3},{5,4},{6,5},{7,6},{4,7},{9,8},{10,9},{11,1... | collective-permute-start | bytes 1160 | tf_op jit(solution)/shard_map/ppermute | solution.py:25
  56.6 1.3 collective-permute-done.3
  57.9 0.0 collective-permute-done.4
  57.9 0.2 collective-permute-start.5
  58.1 6.4 %collective-permute-done.5 = f32[3,3,32]{2,1,0:T(4,128)S(1)} collective-permute-done((f32[3,3,32]{2,1,0:T(4,128)S(1)}, f32[3,3,32]{2,1,0:T(4,128)S(1)}, u32[]{:S(2)}, u32[]{:S(2)}) %collective-permute-start.5) | collective-permute-done | bytes 1184 | tf_op jit(solution)/shard_map/ppermute | solution.py:25
  64.6 0.9 fusion.7
  65.5 0.1 copy.22
  65.6 0.7 gather_fusion.1
  66.3 0.1 copy.23
  66.4 2.1 %collective-permute-start.6 = (f32[3,3,32]{2,1,0:T(4,128)S(1)}, f32[3,3,32]{2,1,0:T(4,128)S(1)}, u32[]{:S(2)}, u32[]{:S(2)}) collective-permute-start(f32[3,3,32]{2,1,0:T(4,128)S(1)} %pad_maximum_fusion.5), channel_id=1, source_target_pairs={{4,0},{8,4},{12,8},{16,12},{20,16},{24,20},{28,24},{0,28},{5,1},{9... | collective-permute-start | bytes 3464 | tf_op jit(solution)/shard_map/ppermute | solution.py:25
  68.5 1.6 %collective-permute-done.6 = f32[3,3,32]{2,1,0:T(4,128)S(1)} collective-permute-done((f32[3,3,32]{2,1,0:T(4,128)S(1)}, f32[3,3,32]{2,1,0:T(4,128)S(1)}, u32[]{:S(2)}, u32[]{:S(2)}) %collective-permute-start.6) | collective-permute-done | bytes 1184 | tf_op jit(solution)/shard_map/ppermute | solution.py:25
  70.1 0.1 collective-permute-start.7
  70.2 0.5 collective-permute-start.8
  70.7 0.6 copy.25
  71.2 2.0 %collective-permute-done.8 = f32[3,32]{1,0:T(4,128)S(1)} collective-permute-done((f32[3,32]{1,0:T(4,128)S(1)}, f32[3,32]{1,0:T(4,128)S(1)}, u32[]{:S(2)}, u32[]{:S(2)}) %collective-permute-start.8) | collective-permute-done | bytes 416 | tf_op jit(solution)/shard_map/ppermute | solution.py:25
  73.2 0.0 collective-permute-done.7
  73.3 0.1 reshape.66
  73.3 0.6 select_maximum_fusion.residual
  74.0 19.2 %edge_backward.1 = f32[4,832,128]{2,1,0:T(8,128)} custom-call(s32[1,1]{1,0:T(1,128)S(6)} %copy.33.live, s32[1,2048]{1,0:T(1,128)} %bitcast.56, f32[8,2048]{1,0:T(8,128)} %pad.8.vec, f32[256,128]{1,0:T(8,128)} %pad_maximum_fusion.table, f32[8,256]{1,0:T(8,128)} %select_maximum_fusion.residual, bf16[8,512,256]{2,1,0:T(8,128)(2,1)} %get-tuple-element.22.m1, ...), custom_call_target="tpu_custom_call" | custom-call | tf_op jit(solution)/shard_map/edge_backward/pallas_call | solution.py:494
  93.1 42.7 %sum_grads.1 = f32[2,2,2,4,104,128]{5,4,3,2,1,0:T(8,128)} custom-call(f32[2,2,2,4,104,128]{5,4,3,2,1,0:T(8,128)} %bitcast.46), custom_call_target="tpu_custom_call" | custom-call | tf_op jit(solution)/shard_map/sum_grads/pallas_call | solution.py:337
  135.9 2.6 %unpack_grads.1 = (f32[128,512]{1,0:T(8,128)}, f32[128,512]{1,0:T(8,128)}, f32[512,512]{1,0:T(8,128)}, f32[16,512]{1,0:T(8,128)}, f32[8,512]{1,0:T(8,128)}, /*index=5*/f32[8,512]{1,0:T(8,128)}) custom-call(f32[4,832,128]{2,1,0:T(8,128)} %bitcast.45), custom_call_target="tpu_custom_call" | custom-call | tf_op jit(solution)/shard_map/unpack_grads/pallas_call | solution.py:517
  138.5 1.3 slice.101
  (22 shorter events, 0.1 us)
Async XLA Ops:
  3.7 7.8 %collective-permute-start = (f32[3,32,128]{2,1,0:T(8,128)S(1)}, f32[3,32,128]{2,1,0:T(8,128)S(1)}, u32[]{:S(2)}, u32[]{:S(2)}) collective-permute-start(f32[3,32,128]{2,1,0:T(8,128)S(1)} %pad_maximum_fusion.2), channel_id=1, source_target_pairs={{4,0},{8,4},{12,8},{16,12},{20,16},{24,20},{28,24},{0,28},{5,1},{9... | collective-permute-start | bytes 147464 | tf_op jit(solution)/shard_map/ppermute | solution.py:25
  11.5 3.5 %collective-permute-start.1 = (f32[2,32,128]{2,1,0:T(8,128)S(1)}, f32[2,32,128]{2,1,0:T(8,128)S(1)}, u32[]{:S(2)}, u32[]{:S(2)}) collective-permute-start(f32[2,32,128]{2,1,0:T(8,128)S(1)} %pad_maximum_fusion.3), channel_id=1, source_target_pairs={{1,0},{2,1},{3,2},{0,3},{5,4},{6,5},{7,6},{4,7},{9,8},{10,9},{11,1... | collective-permute-start | bytes 98312 | tf_op jit(solution)/shard_map/ppermute | solution.py:25
  11.7 3.3 %collective-permute-start.2 = (f32[32,128]{1,0:T(8,128)S(1)}, f32[32,128]{1,0:T(8,128)S(1)}, u32[]{:S(2)}, u32[]{:S(2)}) collective-permute-start(f32[32,128]{1,0:T(8,128)S(1)} %get-tuple-element.45), channel_id=1, source_target_pairs={{3,0},{0,1},{1,2},{2,3},{7,4},{4,5},{5,6},{6,7},{11,8},{8,9},{9,10... | collective-permute-start | bytes 49160 | tf_op jit(solution)/shard_map/ppermute | solution.py:25
  54.9 3.1 %collective-permute-start.3 = (f32[2,3,32]{2,1,0:T(4,128)S(1)}, f32[2,3,32]{2,1,0:T(4,128)S(1)}, u32[]{:S(2)}, u32[]{:S(2)}) collective-permute-start(f32[2,3,32]{2,1,0:T(4,128)S(1)} %stack.53), channel_id=1, source_target_pairs={{3,0},{0,1},{1,2},{2,3},{7,4},{4,5},{5,6},{6,7},{11,8},{8,9},{9,10... | collective-permute-start | bytes 2312 | tf_op jit(solution)/shard_map/ppermute | solution.py:25
  55.2 2.7 %collective-permute-start.4 = (f32[3,32]{1,0:T(4,128)S(1)}, f32[3,32]{1,0:T(4,128)S(1)}, u32[]{:S(2)}, u32[]{:S(2)}) collective-permute-start(f32[3,32]{1,0:T(4,128)S(1)} %get-tuple-element.50), channel_id=1, source_target_pairs={{1,0},{2,1},{3,2},{0,3},{5,4},{6,5},{7,6},{4,7},{9,8},{10,9},{11,1... | collective-permute-start | bytes 1160 | tf_op jit(solution)/shard_map/ppermute | solution.py:25
  57.9 6.6 %collective-permute-start.5 = (f32[3,3,32]{2,1,0:T(4,128)S(1)}, f32[3,3,32]{2,1,0:T(4,128)S(1)}, u32[]{:S(2)}, u32[]{:S(2)}) collective-permute-start(f32[3,3,32]{2,1,0:T(4,128)S(1)} %pad_maximum_fusion.4), channel_id=1, source_target_pairs={{28,0},{0,4},{4,8},{8,12},{12,16},{16,20},{20,24},{24,28},{29,1},{... | collective-permute-start | bytes 3464 | tf_op jit(solution)/shard_map/ppermute | solution.py:25
  66.4 3.7 %collective-permute-start.6 = (f32[3,3,32]{2,1,0:T(4,128)S(1)}, f32[3,3,32]{2,1,0:T(4,128)S(1)}, u32[]{:S(2)}, u32[]{:S(2)}) collective-permute-start(f32[3,3,32]{2,1,0:T(4,128)S(1)} %pad_maximum_fusion.5), channel_id=1, source_target_pairs={{4,0},{8,4},{12,8},{16,12},{20,16},{24,20},{28,24},{0,28},{5,1},{9... | collective-permute-start | bytes 3464 | tf_op jit(solution)/shard_map/ppermute | solution.py:25
  70.1 3.1 %collective-permute-start.7 = (f32[2,3,32]{2,1,0:T(4,128)S(1)}, f32[2,3,32]{2,1,0:T(4,128)S(1)}, u32[]{:S(2)}, u32[]{:S(2)}) collective-permute-start(f32[2,3,32]{2,1,0:T(4,128)S(1)} %pad_maximum_fusion.6), channel_id=1, source_target_pairs={{1,0},{2,1},{3,2},{0,3},{5,4},{6,5},{7,6},{4,7},{9,8},{10,9},{11,1... | collective-permute-start | bytes 2312 | tf_op jit(solution)/shard_map/ppermute | solution.py:25
  70.2 3.1 %collective-permute-start.8 = (f32[3,32]{1,0:T(4,128)S(1)}, f32[3,32]{1,0:T(4,128)S(1)}, u32[]{:S(2)}, u32[]{:S(2)}) collective-permute-start(f32[3,32]{1,0:T(4,128)S(1)} %get-tuple-element.52), channel_id=1, source_target_pairs={{3,0},{0,1},{1,2},{2,3},{7,4},{4,5},{5,6},{6,7},{11,8},{8,9},{9,10... | collective-permute-start | bytes 1160 | tf_op jit(solution)/shard_map/ppermute | solution.py:25

commit v2 on v1

--- a/solution.py
+++ b/solution.py
@@ -19,40 +19,86 @@
 BF16 = jnp.bfloat16
 
 
-def passed_along(block, axis, distance):
-    devices = range(lax.axis_size(axis))
-    route = [((i - distance) % len(devices), i) for i in devices]
-    return lax.ppermute(block, axis, route)
-
-
-def pull_x(value):
-    return passed_along(value, "bx", -1)
-
-
-def push_x(value):
-    return passed_along(value, "bx", 1)
-
-
-def pull_y(value):
-    return passed_along(value, "by", -1)
-
-
-def push_y(value):
-    return passed_along(value, "by", 1)
-
-
-def fetch_ghosts(rows):
-    across = pull_x(jnp.stack([rows[0], rows[2], rows[3]]))
-    upper = pull_y(jnp.stack([rows[1], across[1]]))
-    lower = push_y(across[2])
-    return jnp.stack([across[0], upper[0], upper[1], lower])
-
-
-def return_partials(parts):
-    upper = push_y(jnp.stack([parts[1], parts[2]]))
-    lower = pull_y(parts[3])
-    across = push_x(jnp.stack([parts[0], upper[1], lower]))
-    return jnp.stack([across[0], upper[0], across[1], across[2]])
+DIRECTIONS = ((1, 0), (0, 1), (1, 1), (1, -1))
+
+
+def greet():
+    nbx, nby = lax.axis_size("bx"), lax.axis_size("by")
+    bx, by = lax.axis_index("bx"), lax.axis_index("by")
+    above = [(lax.rem(bx + dx, nbx), lax.rem(by + dy + nby, nby)) for dx, dy in DIRECTIONS]
+    below = [(lax.rem(bx - dx + nbx, nbx), lax.rem(by - dy + nby, nby)) for dx, dy in DIRECTIONS]
+    barrier = pltpu.get_barrier_semaphore()
+    for device in above + below:
+        pl.semaphore_signal(barrier, inc=1, device_id=device, device_id_type=MESH)
+    pl.semaphore_wait(barrier, len(above + below))
+    return above, below
+
+
+def remote(src, dst, send, recv, device):
+    copy = pltpu.make_async_remote_copy(
+        src_ref=src, dst_ref=dst, send_sem=send, recv_sem=recv,
+        device_id=device, device_id_type=MESH,
+    )
+    copy.start()
+    return copy
+
+
+def fetch_rows(features, sends, table, lent, send, recv):
+    atoms = features.shape[0]
+    ghosts = lent.shape[0] // len(DIRECTIONS)
+    spots = lax.broadcasted_iota(jnp.int32, (atoms, lent.shape[0]), 0) == sends[...]
+    spots = jnp.where(spots, 1.0, 0.0).T
+    lent[...] = jnp.dot(spots, features[...], precision=HIGHEST, preferred_element_type=F32)
+    table[0:atoms, :] = features[...]
+    _, below = greet()
+    copies = [
+        remote(
+            lent.at[pl.ds(d * ghosts, ghosts)], table.at[pl.ds(atoms + d * ghosts, ghosts)],
+            send.at[d], recv.at[d], below[d],
+        )
+        for d in range(len(DIRECTIONS))
+    ]
+    for copy in copies:
+        copy.wait()
+
+
+def settle(ext, sends, target, forces, table, part, came, lent, back, send, recv):
+    atoms = target.shape[1]
+    count = part.shape[1]
+    ghosts = count // len(DIRECTIONS)
+    part[...] = ext[:, atoms:]
+    above, below = greet()
+    copies = [
+        remote(part, came.at[d], send.at[d], recv.at[d], above[d]) for d in range(len(DIRECTIONS))
+    ]
+    spots = lax.broadcasted_iota(jnp.int32, (atoms, count), 0) == sends[...]
+    spots = jnp.where(spots, 1.0, 0.0)
+    lane = lax.broadcasted_iota(jnp.int32, part.shape, 1)
+
+    def gathered(blocks):
+        total = blocks[0]
+        for d in range(1, len(DIRECTIONS)):
+            total = jnp.where(lane >= d * ghosts, blocks[d], total)
+        return total
+
+    for copy in copies:
+        copy.wait()
+    returned = lax.dot_general(
+        gathered(came), spots, (((1,), (1,)), ((), ())),
+        precision=HIGHEST, preferred_element_type=F32,
+    )
+    force = ext[:, 0:atoms] + returned
+    forces[...] = force
+    residual = (force - target[...]) / atoms
+    table[:, 0:atoms] = residual
+    lent[...] = jnp.dot(residual, spots, precision=HIGHEST, preferred_element_type=F32)
+    copies = [
+        remote(lent, back.at[d], send.at[4 + d], recv.at[4 + d], below[d])
+        for d in range(len(DIRECTIONS))
+    ]
+    for copy in copies:
+        copy.wait()
+    table[:, atoms:] = gathered(back)
 
 
 def split(x):
@@ -95,7 +141,7 @@
     extent, width = table.shape
     hidden = w_mid.shape[0]
     nb, ns = w_radial.shape[0], species_table.shape[0]
-    pb = first.shape[1]
+    pb = first.shape[1] // 2
     base = atoms + extent
     used = base + 2 * nb + ns
 
@@ -113,63 +159,107 @@
         wo[...] = jnp.broadcast_to(w_out[...], (pb, hidden)).T
         ext[...] = jnp.zeros_like(ext)
 
-    square = jnp.sum(vec[...] * vec[...], axis=0, keepdims=True) + 1.0
-    radius = jnp.sqrt(square)
-    order = (lax.broadcasted_iota(jnp.int32, (nb, pb), 0) + 1).astype(F32) * (math.pi / RCUT)
-    phase = order * radius
-    sine, cosine = jnp.sin(phase), jnp.cos(phase)
-    basis = sine / radius
-    slope_basis = (order * cosine / radius - sine / square) / radius
-    basis_hi = basis.astype(BF16).astype(F32)
-    slope_hi = slope_basis.astype(BF16).astype(F32)
-    m1[0:atoms, :] = onehot(first[...], atoms, pb)
-    m1[atoms:base, :] = onehot(second[...], extent, pb)
-    m1[base : base + 2 * nb, :] = jnp.concatenate([basis_hi, basis - basis_hi], axis=0).astype(BF16)
-    m1[base + 2 * nb : used, :] = onehot(species[...], ns, pb)
-    m1[used:, :] = jnp.zeros((m1.shape[0] - used, pb), BF16)
-    mt[0 : 2 * nb, :] = jnp.concatenate([slope_hi, slope_basis - slope_hi], axis=0).astype(BF16)
-    mt[2 * nb :, :] = jnp.zeros((mt.shape[0] - 2 * nb, pb), BF16)
-
-    za[...] = mm(c_hi[...], m1[...]) + mm(c_lo[...], m1[...])
-    ta[...] = mm(c_hi[:, base:], mt[...]) + mm(c_lo[:, base:], mt[...])
-    for i in range(0, hidden, CHUNK):
-        rows = slice(i, i + CHUNK)
-        z, t = za[rows, :], ta[rows, :]
-        act, d1, d2 = slopes_of(z)
-        za[rows, :] = d1
-        ta[rows, :] = d2 * t
-        u_hi[rows, 0:pb], u_lo[rows, 0:pb] = split(act)
-        u_hi[rows, pb:], u_lo[rows, pb:] = split(d1 * t)
-    md[...] = mm(wt_hi[...], u_hi[...]) + mm(wt_lo[...], u_hi[...]) + mm(wt_hi[...], u_lo[...])
-    slope = jnp.zeros((1, pb), F32)
-    for i in range(0, hidden, CHUNK):
-        rows = slice(i, i + CHUNK)
-        m, dm, out = md[rows, 0:pb], md[rows, pb:], wo[rows, :]
-        _, d1, d2 = slopes_of(m)
-        x = d1 * dm
-        xs[rows, :] = x
-        slope = slope + jnp.sum(out * x, axis=0, keepdims=True)
-        e, g = out * d2 * dm, out * d1
-        eg[rows, 0:pb] = e
-        eg[rows, pb:] = g
-        eg_hi[rows, 0:pb], eg_lo[rows, 0:pb] = split(e)
-        eg_hi[rows, pb:], eg_lo[rows, pb:] = split(g)
-    md[...] = mm(w_hi[...], eg_hi[...]) + mm(w_lo[...], eg_hi[...]) + mm(w_hi[...], eg_lo[...])
-    for i in range(0, hidden, CHUNK):
-        rows = slice(i, i + CHUNK)
-        e, g, d1 = md[rows, 0:pb], md[rows, pb:], za[rows, :]
-        zt[rows, 0:pb] = e * d1 + g * ta[rows, :]
-        zt[rows, pb:] = g * d1
-    slots = step * pb + lax.broadcasted_iota(jnp.int32, (1, pb), 1)
-    coupling = jnp.where(slots < live[0, 0], slope, 0.0)
-    pushed = coupling * vec[...]
-    pushed_hi = pushed.astype(BF16).astype(F32)
-    pushed2 = jnp.concatenate([pushed_hi, pushed - pushed_hi], axis=0).astype(BF16)
-    half = pushed.shape[0]
-    on_first = mm_t(pushed2, m1[0:atoms, :])
-    on_second = mm_t(pushed2, m1[atoms:base, :])
-    ext[:, 0:atoms] += on_first[0:half] + on_first[half:]
-    ext[...] -= on_second[0:half] + on_second[half:]
+    rows_at = [slice(i, i + hidden // 2) for i in range(0, hidden, hidden // 2)]
+    chunks = [[slice(i, i + CHUNK) for i in range(r.start, r.stop, CHUNK)] for r in rows_at]
+    slopes = [jnp.zeros((1, pb), F32), jnp.zeros((1, pb), F32)]
+
+    def lanes_of(k):
+        return slice(k * pb, (k + 1) * pb)
+
+    def prepare(k):
+        lane = lanes_of(k)
+        square = jnp.sum(vec[:, lane] * vec[:, lane], axis=0, keepdims=True) + 1.0
+        radius = jnp.sqrt(square)
+        order = (lax.broadcasted_iota(jnp.int32, (nb, pb), 0) + 1).astype(F32) * (math.pi / RCUT)
+        phase = order * radius
+        sine, cosine = jnp.sin(phase), jnp.cos(phase)
+        basis = sine / radius
+        slope_basis = (order * cosine / radius - sine / square) / radius
+        basis_hi = basis.astype(BF16).astype(F32)
+        slope_hi = slope_basis.astype(BF16).astype(F32)
+        m1[k, 0:atoms, :] = onehot(first[:, lane], atoms, pb)
+        m1[k, atoms:base, :] = onehot(second[:, lane], extent, pb)
+        m1[k, base : base + 2 * nb, :] = jnp.concatenate([basis_hi, basis - basis_hi], axis=0).astype(BF16)
+        m1[k, base + 2 * nb : used, :] = onehot(species[:, lane], ns, pb)
+        m1[k, used:, :] = jnp.zeros((m1.shape[1] - used, pb), BF16)
+        mt[k, 0 : 2 * nb, :] = jnp.concatenate([slope_hi, slope_basis - slope_hi], axis=0).astype(BF16)
+        mt[k, 2 * nb :, :] = jnp.zeros((mt.shape[1] - 2 * nb, pb), BF16)
+
+    def first_dot(k, r):
+        rows = rows_at[r]
+        za[k, rows, :] = mm(c_hi[rows, :], m1[k]) + mm(c_lo[rows, :], m1[k])
+        ta[k, rows, :] = mm(c_hi[rows, base:], mt[k]) + mm(c_lo[rows, base:], mt[k])
+
+    def first_act(k, r):
+        for rows in chunks[r]:
+            z, t = za[k, rows, :], ta[k, rows, :]
+            act, d1, d2 = slopes_of(z)
+            za[k, rows, :] = d1
+            ta[k, rows, :] = d2 * t
+            u_hi[k, rows, 0:pb], u_lo[k, rows, 0:pb] = split(act)
+            u_hi[k, rows, pb:], u_lo[k, rows, pb:] = split(d1 * t)
+
+    def mid_dot(k, r):
+        rows = rows_at[r]
+        md[k, rows, :] = (
+            mm(wt_hi[rows, :], u_hi[k]) + mm(wt_lo[rows, :], u_hi[k]) + mm(wt_hi[rows, :], u_lo[k])
+        )
+
+    def mid_act(k, r):
+        for rows in chunks[r]:
+            m, dm, out = md[k, rows, 0:pb], md[k, rows, pb:], wo[rows, :]
+            _, d1, d2 = slopes_of(m)
+            x = d1 * dm
+            xs[k, rows, :] = x
+            slopes[k] = slopes[k] + jnp.sum(out * x, axis=0, keepdims=True)
+            e, g = out * d2 * dm, out * d1
+            eg[k, rows, 0:pb] = e
+            eg[k, rows, pb:] = g
+            eg_hi[k, rows, 0:pb], eg_lo[k, rows, 0:pb] = split(e)
+            eg_hi[k, rows, pb:], eg_lo[k, rows, pb:] = split(g)
+
+    def back_dot(k, r):
+        rows = rows_at[r]
+        md[k, rows, :] = (
+            mm(w_hi[rows, :], eg_hi[k]) + mm(w_lo[rows, :], eg_hi[k]) + mm(w_hi[rows, :], eg_lo[k])
+        )
+
+    def back_act(k, r):
+        for rows in chunks[r]:
+            e, g, d1 = md[k, rows, 0:pb], md[k, rows, pb:], za[k, rows, :]
+            zt[k, rows, 0:pb] = e * d1 + g * ta[k, rows, :]
+            zt[k, rows, pb:] = g * d1
+
+    def push(k):
+        slots = (step * 2 + k) * pb + lax.broadcasted_iota(jnp.int32, (1, pb), 1)
+        coupling = jnp.where(slots < live[0, 0], slopes[k], 0.0)
+        pushed = coupling * vec[:, lanes_of(k)]
+        pushed_hi = pushed.astype(BF16).astype(F32)
+        pushed2 = jnp.concatenate([pushed_hi, pushed - pushed_hi], axis=0).astype(BF16)
+        half = pushed.shape[0]
+        on_first = mm_t(pushed2, m1[k, 0:atoms, :])
+        on_second = mm_t(pushed2, m1[k, atoms:base, :])
+        ext[:, 0:atoms] += on_first[0:half] + on_first[half:]
+        ext[...] -= on_second[0:half] + on_second[half:]
+
+    prepare(0)
+    prepare(1)
+    first_dot(0, 0)
+    first_dot(0, 1)
+    for dot, dot_k, act, act_k in (
+        (first_dot, 1, first_act, 0),
+        (mid_dot, 0, first_act, 1),
+        (mid_dot, 1, mid_act, 0),
+        (back_dot, 0, mid_act, 1),
+        (back_dot, 1, back_act, 0),
+    ):
+        for r in range(2):
+            dot(dot_k, r)
+            act(act_k, r)
+    push(0)
+    back_act(1, 0)
+    back_act(1, 1)
+    push(1)
 
 
 def phase_two(
@@ -180,8 +270,8 @@
 ):
     step = pl.program_id(0)
     extent, width = table.shape
-    hidden = u_hi.shape[0]
-    pb = first.shape[1]
+    hidden = u_hi.shape[1]
+    pb = first.shape[1] // 2
     base = atoms + extent
 
     @pl.when(step == 0)
@@ -195,24 +285,48 @@
     res_hi = res.astype(BF16).astype(F32)
     res2 = jnp.concatenate([res_hi, res - res_hi], axis=0).astype(BF16)
     half = res.shape[0]
-    apart = mm(res2[:, 0:atoms], m1[0:atoms, :]) - mm(res2, m1[atoms:base, :])
-    slots = step * pb + lax.broadcasted_iota(jnp.int32, (1, pb), 1)
-    pulled = jnp.sum((apart[0:half] + apart[half:]) * vec[...], axis=0, keepdims=True)
-    weight = jnp.where(slots < live[0, 0], pulled, 0.0)
-    for i in range(0, hidden, CHUNK):
-        rows = slice(i, i + CHUNK)
-        we_hi[rows, 0:pb], we_lo[rows, 0:pb] = split(eg[rows, 0:pb] * weight)
-        we_hi[rows, pb:], we_lo[rows, pb:] = split(eg[rows, pb:] * weight)
-        zh[rows, :], zl[rows, :] = split(zt[rows, 0:pb] * weight)
-        th[rows, :], tl[rows, :] = split(zt[rows, pb:] * weight)
-        x = xs[rows, :] * weight
-        total = d_out[rows, :]
-        for j in range(0, pb, LANES):
-            total = total + x[:, j : j + LANES]
-        d_out[rows, :] = total
-    d_mid[...] += mm_t(u_hi[...], we_hi[...]) + mm_t(u_lo[...], we_hi[...]) + mm_t(u_hi[...], we_lo[...])
-    d_wide[...] += mm_t(m1[...], zh[...]) + mm_t(m1[...], zl[...])
-    d_slope[...] += mm_t(mt[0 : 2 * nb, :], th[...]) + mm_t(mt[0 : 2 * nb, :], tl[...])
+
+    def weigh(k):
+        apart = mm(res2[:, 0:atoms], m1[k, 0:atoms, :]) - mm(res2, m1[k, atoms:base, :])
+        slots = (step * 2 + k) * pb + lax.broadcasted_iota(jnp.int32, (1, pb), 1)
+        moved = (apart[0:half] + apart[half:]) * vec[:, k * pb : (k + 1) * pb]
+        return jnp.where(slots < live[0, 0], jnp.sum(moved, axis=0, keepdims=True), 0.0)
+
+    def scale(k, r, weight):
+        for i in range(r * hidden // 2, (r + 1) * hidden // 2, CHUNK):
+            rows = slice(i, i + CHUNK)
+            we_hi[k, rows, 0:pb], we_lo[k, rows, 0:pb] = split(eg[k, rows, 0:pb] * weight)
+            we_hi[k, rows, pb:], we_lo[k, rows, pb:] = split(eg[k, rows, pb:] * weight)
+            zh[k, rows, :], zl[k, rows, :] = split(zt[k, rows, 0:pb] * weight)
+            th[k, rows, :], tl[k, rows, :] = split(zt[k, rows, pb:] * weight)
+            x = xs[k, rows, :] * weight
+            total = d_out[rows, :]
+            for j in range(0, pb, LANES):
+                total = total + x[:, j : j + LANES]
+            d_out[rows, :] = total
+
+    def contract(k, r):
+        rows = slice(r * hidden // 2, (r + 1) * hidden // 2)
+        d_mid[rows, :] += (
+            mm_t(u_hi[k, rows, :], we_hi[k]) + mm_t(u_lo[k, rows, :], we_hi[k])
+            + mm_t(u_hi[k, rows, :], we_lo[k])
+        )
+        rows = slice(r * m1.shape[1] // 2, (r + 1) * m1.shape[1] // 2)
+        d_wide[rows, :] += mm_t(m1[k, rows, :], zh[k]) + mm_t(m1[k, rows, :], zl[k])
+
+    def contract_slope(k):
+        d_slope[...] += mm_t(mt[k, 0 : 2 * nb, :], th[k]) + mm_t(mt[k, 0 : 2 * nb, :], tl[k])
+
+    weights = [weigh(0), weigh(1)]
+    scale(0, 0, weights[0])
+    scale(0, 1, weights[0])
+    for r in range(2):
+        contract(0, r)
+        scale(1, r, weights[1])
+    contract_slope(0)
+    contract(1, 0)
+    contract(1, 1)
+    contract_slope(1)
 
     @pl.when(step == pl.num_programs(0) - 1)
     def _():
@@ -385,13 +499,25 @@
     nb, ns = w_radial.shape[0], species_table.shape[0]
     pairs = first.shape[1]
     pb = min(PBLOCK, pairs)
-    steps = pairs // pb
+    steps = pairs // (2 * pb)
     deep = round_up(atoms + extent + 2 * nb + ns, LANES)
     thin = deep - atoms - extent
 
-    lent = jnp.take(local_feat, sends, axis=0)
-    arrived = fetch_ghosts(lent)
-    table = jnp.concatenate([local_feat, arrived.reshape(4 * ghosts, width)], axis=0)
+    sends = sends.reshape(1, 4 * ghosts)
+    whole = pl.BlockSpec(memory_space=pltpu.VMEM)
+    table = pl.pallas_call(
+        fetch_rows,
+        out_shape=jax.ShapeDtypeStruct((extent, width), F32),
+        in_specs=[whole, whole],
+        out_specs=whole,
+        scratch_shapes=[
+            pltpu.VMEM((4 * ghosts, width), F32),
+            pltpu.SemaphoreType.DMA((4,)),
+            pltpu.SemaphoreType.DMA((4,)),
+        ],
+        compiler_params=pltpu.CompilerParams(collective_id=2, has_side_effects=True),
+        name="fetch_rows",
+    )(local_feat, sends)
 
     smem = pl.BlockSpec(memory_space=pltpu.SMEM)
 
@@ -399,13 +525,13 @@
         return pl.BlockSpec(dims, lambda i: (0,) * len(dims))
 
     def lane_block(rows):
-        return pl.BlockSpec((rows, pb), lambda i: (0, i))
+        return pl.BlockSpec((rows, 2 * pb), lambda i: (0, i))
 
     def step_block(rows, cols):
-        return pl.BlockSpec((None, rows, cols), lambda i: (i, 0, 0))
+        return pl.BlockSpec((2, rows, cols), lambda i: (i, 0, 0))
 
     def stacked(rows, cols, dtype):
-        return jax.ShapeDtypeStruct((steps, rows, cols), dtype)
+        return jax.ShapeDtypeStruct((2 * steps, rows, cols), dtype)
 
     params = pltpu.CompilerParams(
         dimension_semantics=("arbitrary",), vmem_limit_bytes=VMEM_BYTES
@@ -455,11 +581,11 @@
             pltpu.VMEM((hidden, hidden), BF16),
             pltpu.VMEM((hidden, hidden), BF16),
             pltpu.VMEM((hidden, pb), F32),
-            pltpu.VMEM((hidden, pb), F32),
-            pltpu.VMEM((hidden, pb), F32),
-            pltpu.VMEM((hidden, 2 * pb), F32),
-            pltpu.VMEM((hidden, 2 * pb), BF16),
-            pltpu.VMEM((hidden, 2 * pb), BF16),
+            pltpu.VMEM((2, hidden, pb), F32),
+            pltpu.VMEM((2, hidden, pb), F32),
+            pltpu.VMEM((2, hidden, 2 * pb), F32),
+            pltpu.VMEM((2, hidden, 2 * pb), BF16),
+            pltpu.VMEM((2, hidden, 2 * pb), BF16),
             pltpu.VMEM((deep, hidden), F32),
         ],
         compiler_params=params,
@@ -468,17 +594,25 @@
         live_pairs, first, second, species, vec, table, w_a, w_b, w_radial, species_table, w_mid,
         w_out[None],
     )
-    extended = ext[:3]
-    parts = jnp.transpose(extended[:, atoms:].reshape(3, 4, ghosts), (1, 0, 2))
-    returned = return_partials(parts)
-    spots = (sends[:, :, None] == jnp.arange(atoms)[None, None, :]).astype(jnp.float32)
-    forces = extended[:, :atoms] + jnp.einsum("dcg,dga->ca", returned, spots, precision=HIGHEST)
-    residual = (forces - target) / atoms
-    residual_lent = jnp.transpose(jnp.take(residual, sends, axis=1), (1, 0, 2))
-    residual_ghosts = fetch_ghosts(residual_lent)
-    residual_table = jnp.concatenate(
-        [residual, jnp.transpose(residual_ghosts, (1, 0, 2)).reshape(3, 4 * ghosts)], axis=1
-    )
+    forces, residual_table = pl.pallas_call(
+        settle,
+        out_shape=[
+            jax.ShapeDtypeStruct((8, atoms), F32),
+            jax.ShapeDtypeStruct((8, extent), F32),
+        ],
+        in_specs=[whole, whole, whole],
+        out_specs=[whole, whole],
+        scratch_shapes=[
+            pltpu.VMEM((8, 4 * ghosts), F32),
+            pltpu.VMEM((4, 8, 4 * ghosts), F32),
+            pltpu.VMEM((8, 4 * ghosts), F32),
+            pltpu.VMEM((4, 8, 4 * ghosts), F32),
+            pltpu.SemaphoreType.DMA((8,)),
+            pltpu.SemaphoreType.DMA((8,)),
+        ],
+        compiler_params=pltpu.CompilerParams(collective_id=3, has_side_effects=True),
+        name="settle_forces",
+    )(ext, sends, jnp.pad(target, ((0, 5), (0, 0))))
 
     nbx, nby = lax.axis_size("bx"), lax.axis_size("by")
     gx = 2 if nbx % 2 == 0 else 1
@@ -499,12 +633,12 @@
         + kept_specs,
         out_specs=full(columns, tall, LANES),
         scratch_shapes=[
-            pltpu.VMEM((hidden, 2 * pb), BF16),
-            pltpu.VMEM((hidden, 2 * pb), BF16),
-            pltpu.VMEM((hidden, pb), BF16),
-            pltpu.VMEM((hidden, pb), BF16),
-            pltpu.VMEM((hidden, pb), BF16),
-            pltpu.VMEM((hidden, pb), BF16),
+            pltpu.VMEM((2, hidden, 2 * pb), BF16),
+            pltpu.VMEM((2, hidden, 2 * pb), BF16),
+            pltpu.VMEM((2, hidden, pb), BF16),
+            pltpu.VMEM((2, hidden, pb), BF16),
+            pltpu.VMEM((2, hidden, pb), BF16),
+            pltpu.VMEM((2, hidden, pb), BF16),
             pltpu.VMEM((hidden, hidden), F32),
             pltpu.VMEM((deep, hidden), F32),
             pltpu.VMEM((2 * nb, hidden), F32),
@@ -512,7 +646,7 @@
         ],
         compiler_params=params,
         name="edge_backward",
-    )(live_pairs, first, vec, table, jnp.pad(residual_table, ((0, 5), (0, 0))), *kept)
+    )(live_pairs, first, vec, table, residual_table, *kept)
     summed = sum_everywhere(packed, sizes, rows).reshape(columns, tall, LANES)
     outs = pl.pallas_call(
         unpack,
@@ -523,7 +657,7 @@
         name="unpack_grads",
     )(summed)
     d_a, d_b, d_mid, d_species, d_radial, d_out = outs
-    return (forces[None, None], d_a, d_b, d_radial, d_species, d_mid, d_out[0])
+    return (forces[None, None, 0:3], d_a, d_b, d_radial, d_species, d_mid, d_out[0])
 
 
 def solution(mesh):

time: 140 us -> 120 us (0.86)
  waiting for transfers between devices: 14 us -> 0 us
  starting transfers between devices: 11.2 us -> 0 us
  Pallas kernels: 102 us -> 111 us
  other arithmetic: 3.63 us -> 0 us
    pallas_call x0 -> x2, Pallas kernels: none -> 23.5 us  [the longest x1 13.2 us: local(): pl.pallas_call(settle, out_shape=[jax.ShapeDtypeStruct((8, atoms), F32),...]
    ppermute x9 -> x0, waiting for transfers between devices: 14 us -> none  [passed_along(): return lax.ppermute(block, axis, route)]
    pallas_call x1, Pallas kernels: 37.5 us -> 25.8 us  [local(): pl.pallas_call(functools.partial(phase_one, atoms), grid=(steps,), out_sh...]
    ppermute x9 -> x0, starting transfers between devices: 11.2 us -> none  [passed_along(): return lax.ppermute(block, axis, route)]
    gather x3 -> x0, local copies, waits for them, and re-layouts: 2.23 us -> none  [the longest x1 1.48 us: local(): lent = jnp.take(local_feat, sends, axis=0)]
    concatenate x2 -> x0, other arithmetic: 2.11 us -> none  [the longest x1 1.51 us: local(): jnp.concatenate([local_feat, arrived.reshape(4 * ghosts, width)], axis=0)]
    pallas_call x1, Pallas kernels: 42.7 us -> 41.2 us  [sum_everywhere(): pl.pallas_call(functools.partial(sum_kernel, sizes, cut), out_shape=jax.S...]
  transfers between devices with their start and end apart: 9 -> 0, of which waited for: 6 -> 0; matrix products, arithmetic and copies ran while one was open for 1% -> 0% of each run, Pallas kernels for 0% -> 0%
where the time goes in v2:
time: 120 us; the launch traced here: 119 us
  Pallas kernels  111 us (92%)
  local copies, waits for them, and re-layouts  6.49 us (5%)
  between operations  1.31 us (1%)
    pallas_call x1, Pallas kernels, sum_everywhere(): pl.pallas_call(functools.partial(sum_kernel, sizes, cut), out_shape=jax.S...  41.2 us
    pallas_call x1, Pallas kernels, local(): pl.pallas_call(functools.partial(phase_one, atoms), grid=(steps,), out_sh...  25.8 us
    pallas_call x1, Pallas kernels, local(): pl.pallas_call(functools.partial(phase_two, atoms, nb, ns), grid=(steps,)...  18.2 us
    pallas_call x1, Pallas kernels, local(): pl.pallas_call(settle, out_shape=[jax.ShapeDtypeStruct((8, atoms), F32),...  13.2 us
    pallas_call x1, Pallas kernels, local(): pl.pallas_call(fetch_rows, out_shape=jax.ShapeDtypeStruct((extent, width)...  10.3 us
    pallas_call x1, Pallas kernels, local(): pl.pallas_call(unpack, out_shape=[jax.ShapeDtypeStruct((n, hidden), F32)...  2.64 us

profile of v2, /device:TPU:0, one launch (start us, length us, event | category | flops | bytes accessed | tf_op | source)
XLA Modules:
  0.0 119.1 jit_solution(13462741594315168916)
XLA Ops:
  1.3 0.8 copy.26
  2.0 0.6 pad.8.vec
  2.7 1.3 %reshape_squeeze.3.sends = s32[1,128]{1,0:T(1,128)} reshape(s32[1,1,4,32]{3,2,1,0:T(4,128)} %param.15) | data formatting | bytes 1024 | tf_op jit(solution)/shard_map/reshape;squeeze | solution.py:506
  3.9 10.3 %fetch_rows.1.table = f32[256,128]{1,0:T(8,128)} custom-call(f32[128,128]{1,0:T(8,128)} %bitcast.19, s32[1,128]{1,0:T(1,128)} %reshape_squeeze.3.sends), custom_call_target="tpu_custom_call" | custom-call | tf_op jit(solution)/shard_map/fetch_rows/pallas_call | solution.py:508
  14.3 25.8 %edge_forward.1 = (f32[8,256]{1,0:T(8,128)}, bf16[8,512,256]{2,1,0:T(8,128)(2,1)}, bf16[8,128,256]{2,1,0:T(8,128)(2,1)}, bf16[8,512,512]{2,1,0:T(8,128)(2,1)}, b...) custom-call(s32[1,1]{1,0:T(1,128)S(6)} %copy.28.live, ...), custom_call_target="tpu_custom_call" | custom-call | tf_op jit(solution)/shard_map/edge_forward/pallas_call | solution.py:548
  40.1 0.7 copy.27
  40.7 0.6 pad.9.target
  41.3 13.2 %settle_forces.1 = (f32[8,128]{1,0:T(8,128)}, f32[8,256]{1,0:T(8,128)}) custom-call(f32[8,256]{1,0:T(8,128)} %get-tuple-element.23.ext, s32[1,128]{1,0:T(1,128)} %reshape_squeeze.3.sends, f32[8,128]{1,0:T(8,128)} %pad.9.target), custom_call_target="tpu_custom_call" | custom-call | tf_op jit(solution)/shard_map/settle_forces/pallas_call | solution.py:597
  54.5 0.7 slice_bitcast_fusion
  55.2 0.6 copy.21
  55.8 18.2 %edge_backward.1 = f32[4,832,128]{2,1,0:T(8,128)} custom-call(s32[1,1]{1,0:T(1,128)S(6)} %copy.28.live, s32[1,2048]{1,0:T(1,128)} %bitcast.21, f32[8,2048]{1,0:T(8,128)} %pad.8.vec, f32[256,128]{1,0:T(8,128)} %fetch_rows.1.table, f32[8,256]{1,0:T(8,128)} %get-tuple-element.25.residual, bf16[8,512,256]{2,1,0:T(8,128)(2,1)} %get-tuple-element.26.m1, ...), custom_call_target="tpu_custom_call" | custom-call | tf_op jit(solution)/shard_map/edge_backward/pallas_call | solution.py:628
  74.0 41.2 %sum_grads.1 = f32[2,2,2,4,104,128]{5,4,3,2,1,0:T(8,128)} custom-call(f32[2,2,2,4,104,128]{5,4,3,2,1,0:T(8,128)} %bitcast.17), custom_call_target="tpu_custom_call" | custom-call | tf_op jit(solution)/shard_map/sum_grads/pallas_call | solution.py:451
  115.2 2.6 %unpack_grads.1 = (f32[128,512]{1,0:T(8,128)}, f32[128,512]{1,0:T(8,128)}, f32[512,512]{1,0:T(8,128)}, f32[16,512]{1,0:T(8,128)}, f32[8,512]{1,0:T(8,128)}, /*index=5*/f32[8,512]{1,0:T(8,128)}) custom-call(f32[4,832,128]{2,1,0:T(8,128)} %bitcast.16), custom_call_target="tpu_custom_call" | custom-call | tf_op jit(solution)/shard_map/unpack_grads/pallas_call | solution.py:651
  117.8 1.3 %slice.7 = f32[1,512]{1,0:T(1,128)} slice(f32[8,512]{1,0:T(8,128)} %get-tuple-element.38), slice={[0:1], [0:512]} | slice | bytes 4096 | tf_op jit(solution)/shard_map/slice | solution.py:660
